TPU v7x, 32 devices: a whole 2x2x4 slice. The times are simulated.
32 devices in a mesh: wide: 8 (over z, y), tensor: 4 (over x, core).
Axes of the slice: x: 2, y: 2, z: 4, core: 2. Of those that a mesh axis runs over, the one named last changes fastest.
Arguments:
- queries: bfloat16 [2, 32, 64, 128], P(None, 'wide', 'tensor'), may hold values from -32 to 32
- prefix_keys: bfloat16 [131072, 8, 128], P('wide', 'tensor'), may hold values from -6 to 6
- prefix_values: bfloat16 [131072, 8, 128], P('wide', 'tensor'), may hold values from -6 to 6
- suffix_keys: bfloat16 [32, 4096, 8, 128], P('wide', None, 'tensor'), may hold values from -8 to 8
- suffix_values: bfloat16 [32, 4096, 8, 128], P('wide', None, 'tensor'), may hold values from -6 to 6
- new_keys: bfloat16 [2, 32, 8, 128], P(None, 'wide', 'tensor'), may hold values from -12 to 12
- new_values: bfloat16 [2, 32, 8, 128], P(None, 'wide', 'tensor'), may hold values from -6 to 6
- suffix_lengths: int32 [32], replicated, may hold values from 1 to 4096, as said below
- slot_row: int32 [32], P('wide'), may hold values from 0 to 31, each once
Outputs:
- attended: bfloat16 [2, 32, 64, 128], P(None, 'wide', 'tensor')
Inputs may be any that keep to these rules, and one draw needn't show every extreme that they name: `suffix_lengths`: some continuation has exactly 4096 cached suffix tokens. `slot_row`: each continuation stands in exactly one slot.
All inputs are finite; a program needn't handle non-finite values.
Results may differ from a plain program's by a relative error of at most 0.0049.
Values may be sent and summed in bfloat16 or wider, within the bound.
No kernel may reach another device: no remote copies, remote signals or barrier semaphores. Data moves between devices by JAX's collectives and lax.ppermute only.
A program may use at most 128 MiB of HBM per device.

v0:
```python
import functools
import math

import jax
import jax.numpy as jnp
from jax import lax
from jax.experimental import pallas as pl
from jax.experimental.pallas import tpu as pltpu
from jax.sharding import PartitionSpec as P

LOG2E = 1.4426950408889634
LANES = 128
STEPS = 2
TILE, BAND, MAX_WAVE, STATS = 256, 64, 1024, 16
WIDE_GRANT, GRANT = 57 * 1024 * 1024, 50 * 1024 * 1024
UNROLL, LAG = 8, 1
TOO_LARGE, TOO_SMALL = 2.0**100, 2.0**-60
F32 = jnp.float32
BF16 = jnp.bfloat16


def coarse(x):
    return jnp.floor(jnp.ceil(x) * 0.0625) * 16.0


def out_of_range(totals):
    return jnp.logical_not((jnp.max(totals) < TOO_LARGE) & (jnp.min(totals) > TOO_SMALL))


def fold_lanes(x, op):
    parts = [x[:, at : at + LANES] for at in range(0, x.shape[1], LANES)]
    while len(parts) > 1:
        parts = [op(a, b) for a, b in zip(parts[::2], parts[1::2])] + parts[len(parts) & ~1 :]
    return parts[0]


def scores_of(q, keys):
    return lax.dot_general(q, keys, (((1,), (1,)), ((), ())), preferred_element_type=F32)


def spread(m, columns):
    return jnp.concatenate([m] * (columns // LANES), axis=1)


def prompt_kernel(kv, piece, scale, *refs):
    q_in, k_hbm, v_hbm, _, out_ref = refs[:5]
    q_all, k_all, v_all, k_wide, v_wide, top, acc, k_sem, v_sem = refs[5:]
    sources = q_in.shape[0]
    rows = q_all.shape[0]
    rows_head = rows // kv
    per = rows_head // sources
    group = q_in.shape[3] // kv
    pieces = k_all.shape[0] // piece
    tile_rows = kv * TILE
    per_piece = piece // tile_rows
    tiles = pieces * per_piece
    unroll = math.gcd(tiles, UNROLL)
    wave = math.gcd(rows_head, MAX_WAVE // kv)
    bands = wave // BAND

    def span(i):
        return pl.ds(pl.multiple_of(i * piece, piece), piece)

    def k_copy(i):
        return pltpu.make_async_copy(k_hbm.at[span(i), :], k_all.at[span(i), :], k_sem.at[i])

    def v_copy(i):
        return pltpu.make_async_copy(v_hbm.at[span(i), :], v_all.at[span(i), :], v_sem.at[i])

    def start(i, carry):
        k_copy(i).start()
        v_copy(i).start()
        return carry

    lax.fori_loop(0, pieces, start, 0)

    for s in range(sources):
        q = q_in[s].astype(F32) * scale
        steps, slots, _, _ = q.shape
        for h in range(kv):
            heads = slice(h * group, (h + 1) * group)
            part = [q[t, r, heads] for t in range(steps) for r in range(slots)]
            part = jnp.concatenate(part, axis=0)
            high = part.astype(BF16)
            low = (part - high.astype(F32)).astype(BF16)
            at = h * rows_head + s * per
            q_all[at : at + per, :] = jnp.concatenate([high, low], axis=1)
    top[...] = jnp.zeros_like(top)

    def widen(ref, wide, t):
        rows_in = ref[pl.ds(pl.multiple_of(t * tile_rows, tile_rows), tile_rows), :]
        wide[...] = rows_in.astype(F32)

    def head_of(wide, h):
        return wide[pl.ds(h, TILE, stride=kv), :].astype(BF16)

    def push_keys(h):
        keys = head_of(k_wide, h)
        pltpu.matmul_push_rhs(jnp.concatenate([keys, keys], axis=1), h, 0, transpose=True)

    def push_values(h):
        values = head_of(v_wide, h)
        pltpu.matmul_push_rhs(jnp.concatenate([values, jnp.ones_like(values)], axis=1), h, 1)

    def run_wave(base, first_wave):
        every = [(h, b) for h in range(kv) for b in range(bands)]

        def band(h, b):
            at = h * rows_head + base + b * BAND
            return slice(at, at + BAND)

        def body(*accs):
            scores = dict(zip(every, accs[: kv * bands]))
            sums = dict(zip(every, accs[kv * bands :]))
            if first_wave:
                k_copy(0).wait()
                v_copy(0).wait()
            widen(k_all, k_wide, 0)
            for h in range(kv):
                push_keys(h)
            for h, b in every:
                load = h if b == 0 else None
                pltpu.matmul_acc_lhs(scores[h, b], q_all[band(h, b), :], load)
            widen(k_all, k_wide, 1)
            widen(v_all, v_wide, 0)
            for h in range(kv):
                push_keys(h)
                push_values(h)

            def visit(p, carry):
                if first_wave:
                    for i in range(unroll // per_piece):
                        ahead = (p * unroll + 1) // per_piece + 1 + i

                        @pl.when(ahead < pieces)
                        def _():
                            k_copy(ahead).wait()
                            v_copy(ahead).wait()

                late = []
                for u in range(unroll):
                    t = p * unroll + u
                    widen(k_all, k_wide, jnp.minimum(t + 2, tiles - 1))
                    widen(v_all, v_wide, jnp.minimum(t + 1, tiles - 1))
                    for h, b in every:
                        load = h if b == 0 else None
                        w = jnp.exp2(pltpu.matmul_pop(scores[h, b])).astype(BF16)
                        pltpu.matmul_acc_lhs(scores[h, b], q_all[band(h, b), :], load)
                        late.append((sums[h, b], w, load))
                        if len(late) > LAG:
                            pltpu.matmul_acc_lhs(*late.pop(0))
                        if b == bands // 2:
                            push_keys(h)
                            push_values(h)
                for held in late:
                    pltpu.matmul_acc_lhs(*held)
                return carry

            lax.fori_loop(0, tiles // unroll, visit, 0)
            for at in every:
                acc[band(*at), :] = pltpu.matmul_pop(sums[at])
            for at in every:
                pltpu.matmul_pop(scores[at])
            for held in (scores[0, 0], sums[0, 0]):
                for h in range(kv):
                    pltpu.matmul_acc_lhs(held, q_all[:BAND, :], h)
                pltpu.matmul_pop(held)

        shape = (BAND, 2 * LANES)
        pl.run_scoped(body, *[pltpu.ACC(u)(shape, F32) for u in range(2) for _ in every])

    for base in range(0, rows_head, wave):
        run_wave(base, base == 0)

    def with_running_top():
        top[...] = jnp.full_like(top, -jnp.inf)
        acc[...] = jnp.zeros_like(acc)

        def body(scores, weighted):
            def visit(t, carry):
                widen(k_all, k_wide, t)
                widen(v_all, v_wide, t)
                for h in range(kv):
                    push_keys(h)
                    push_values(h)
                for at in range(0, rows, BAND):
                    band = slice(at, at + BAND)
                    load = at // rows_head if at % rows_head == 0 else None
                    pltpu.matmul_acc_lhs(scores, q_all[band, :], load)
                    s = pltpu.matmul_pop(scores)
                    peak = jnp.max(fold_lanes(s, jnp.maximum), axis=1, keepdims=True)
                    new_top = jnp.maximum(top[band, :], coarse(peak))
                    shrink = jnp.exp2(top[band, :] - new_top)
                    top[band, :] = new_top
                    w = jnp.exp2(s - spread(new_top, TILE))
                    pltpu.matmul_acc_lhs(weighted, w.astype(BF16), load)
                    kept = acc[band, :] * spread(shrink, 2 * LANES)
                    acc[band, :] = kept + pltpu.matmul_pop(weighted)
                return carry

            lax.fori_loop(0, tiles, visit, 0)

        shape = (BAND, 2 * LANES)
        pl.run_scoped(body, pltpu.ACC(0)(shape, F32), pltpu.ACC(1)(shape, F32))

    pl.when(out_of_range(acc[:, LANES:]))(with_running_top)

    def as_rows(x):
        rest = jnp.zeros((LANES - per, LANES), F32)
        return jnp.concatenate([x, rest], axis=0).T[:STATS]

    row = lax.broadcasted_iota(jnp.int32, (STATS, LANES), 0)
    for s in range(sources):
        stats = jnp.zeros((STATS, LANES), F32)
        for h in range(kv):
            at = slice(h * rows_head + s * per, h * rows_head + (s + 1) * per)
            out_ref[s, :per, h * LANES : (h + 1) * LANES] = acc[at, :LANES].astype(BF16)
            sums = as_rows(acc[at, LANES:])
            high = sums.astype(BF16).astype(F32)
            stats = jnp.where(row == h, as_rows(top[at, :]), stats)
            stats = jnp.where(row == 2 + h, high, stats)
            stats = jnp.where(row == 4 + h, sums - high, stats)
        rest = [jnp.zeros_like(stats)] * (kv - 1)
        out_ref[s, per:, :] = jnp.concatenate([stats, *rest], axis=1).astype(BF16)


def prompt_partials(queries, keys, values, after, kv, scale):
    sources, steps, slots, heads, head_dim = queries.shape
    per = steps * slots * (heads // kv)
    assert kv <= 2 and per <= LANES and per % BAND == 0
    rows = sources * per * kv
    piece = math.gcd(keys.shape[0], UNROLL // 2 * kv * TILE)
    away = pl.BlockSpec(memory_space=pl.ANY)
    inside = pl.BlockSpec(memory_space=pltpu.VMEM)
    return pl.pallas_call(
        functools.partial(prompt_kernel, kv, piece, scale),
        in_specs=[inside, away, away, away],
        out_shape=jax.ShapeDtypeStruct((sources, per + STATS, kv * LANES), BF16),
        scratch_shapes=[
            pltpu.VMEM((rows, 2 * LANES), BF16),
            pltpu.VMEM(keys.shape, BF16),
            pltpu.VMEM(values.shape, BF16),
            pltpu.VMEM((kv * TILE, LANES), F32),
            pltpu.VMEM((kv * TILE, LANES), F32),
            pltpu.VMEM((rows, LANES), F32),
            pltpu.VMEM((rows, 2 * LANES), F32),
            pltpu.SemaphoreType.DMA((keys.shape[0] // piece,)),
            pltpu.SemaphoreType.DMA((keys.shape[0] // piece,)),
        ],
        compiler_params=pltpu.CompilerParams(vmem_limit_bytes=GRANT),
        cost_estimate=pl.CostEstimate(
            flops=4 * rows * keys.shape[0] * head_dim,
            bytes_accessed=4 * keys.shape[0] * head_dim,
            transcendentals=rows * keys.shape[0] // kv,
        ),
        name="prompt",
    )(queries, keys, values, after)


def suffix_kernel(kv, scale, first, lengths, slots, *refs):
    q_ref, nk_ref, nv_ref, k_hbm, v_hbm, _ = refs[:6]
    near_ref, q_all, scores, k_all, v_all, k_sem, v_sem = refs[6:]
    acc_ref, top_ref, total_ref = (near_ref.at[i] for i in range(3))
    _, count, rows, _ = near_ref.shape
    group = q_ref.shape[2] // kv
    pieces = k_sem.shape[1]
    piece = k_all.shape[1] // pieces
    half = piece // 2
    used = [kv * lengths[slots[first + r]] for r in range(count)]
    ends, end = [], 0
    for r in range(count):
        end = end + (used[r] + piece - 1) // piece
        ends.append(end)

    def place(i):
        slot, begin, length = 0, 0, used[0]
        for r in range(1, count):
            past = i >= ends[r - 1]
            slot = jnp.where(past, r, slot)
            begin = jnp.where(past, ends[r - 1], begin)
            length = jnp.where(past, used[r], length)
        return slot, i - begin, length

    def span(at):
        return pl.ds(pl.multiple_of(at * piece, piece), piece)

    def k_copy(slot, at):
        return pltpu.make_async_copy(
            k_hbm.at[first + slot, span(at), :], k_all.at[slot, span(at), :], k_sem.at[slot, at]
        )

    def v_copy(slot, at):
        return pltpu.make_async_copy(
            v_hbm.at[first + slot, span(at), :], v_all.at[slot, span(at), :], v_sem.at[slot, at]
        )

    def start(i, carry):
        slot, at, _ = place(i)
        k_copy(slot, at).start()
        v_copy(slot, at).start()
        return carry

    lax.fori_loop(0, end, start, 0)

    head = lax.broadcasted_iota(jnp.int32, (rows, LANES), 0) // (STEPS * group)
    lane = lax.broadcasted_iota(jnp.int32, (rows, LANES), 1)
    foreign = jnp.where(lane % kv == head, 0.0, -jnp.inf)

    def fresh(slot, relative):
        row = lax.broadcasted_iota(jnp.int32, (rows, LANES), 0)
        second_head = row >= STEPS * group
        second_step = (row // group) % 2 == 1
        own, values = [], []
        for j in range(STEPS):
            nk, nv = nk_ref[j, first + slot].astype(F32), nv_ref[j, first + slot].astype(F32)
            key = jnp.where(second_head, nk[kv - 1 : kv], nk[0:1])
            values.append(jnp.where(second_head, nv[kv - 1 : kv], nv[0:1]))
            q = q_all[slot, :rows, :LANES].astype(F32)
            s = jnp.sum(q * key, axis=1, keepdims=True) * scale
            own.append(jnp.broadcast_to(s, (rows, LANES)))
        own[1] = jnp.where(second_step, own[1], -jnp.inf)
        peak = jnp.ceil(jnp.maximum(own[0], own[1])) if relative else jnp.zeros_like(own[0])
        weights = [jnp.exp2(s - peak) for s in own]
        top_ref[slot] = peak
        total_ref[slot] = weights[0] + weights[1]
        acc_ref[slot] = sum(w.astype(BF16).astype(F32) * v for w, v in zip(weights, values))

    for r in range(count):
        q = [q_ref[t, first + r].astype(F32) for t in range(STEPS)]
        wide = jnp.concatenate(
            [q[t][h * group : (h + 1) * group] for h in range(kv) for t in range(STEPS)], axis=0
        )
        none = jnp.zeros_like(wide)
        q_all[r] = jnp.concatenate(
            [jnp.concatenate([wide, none], axis=1), jnp.concatenate([none, wide], axis=1)], axis=0
        ).astype(BF16)
        fresh(r, False)

    def halves(ref, slot, at):
        begin = pl.multiple_of(at * piece, piece)
        parts = [ref[slot, pl.ds(begin, half), :], ref[slot, pl.ds(begin + half, half), :]]
        return jnp.concatenate(parts, axis=1)

    def score(i):
        slot, at, _ = place(i)
        k_copy(slot, at).wait()
        scores[...] = scores_of(q_all[slot], halves(k_all, slot, at))

    score(0)

    def visit(i, carry):
        slot, at, length = place(i)
        v_copy(slot, at).wait()
        column = lax.broadcasted_iota(jnp.int32, scores.shape, 1)
        column += jnp.where(lax.broadcasted_iota(jnp.int32, scores.shape, 0) >= rows, half, 0)
        bias = spread(jnp.concatenate([foreign, foreign], axis=0), half)
        s = jnp.where(column < length - at * piece, scores[...] * scale + bias, -jnp.inf)
        pl.when(i + 1 < end)(lambda: score(i + 1))
        w = jnp.exp2(s)
        sums = jnp.sum(fold_lanes(w, jnp.add), axis=1, keepdims=True)
        total_ref[slot] += jnp.broadcast_to(sums[:rows] + sums[rows:], (rows, LANES))
        out = jnp.dot(w.astype(BF16), halves(v_all, slot, at), preferred_element_type=F32)
        acc_ref[slot] += out[:rows, :LANES] + out[rows:, LANES:]
        return carry

    lax.fori_loop(0, end, visit, 0)

    def with_running_top(slot):
        fresh(slot, True)
        some = 512

        def visit(i, carry):
            begin = pl.multiple_of(i * some, some)
            keys, values = k_all[slot, pl.ds(begin, some), :], v_all[slot, pl.ds(begin, some), :]
            s = scores_of(q_all[slot, :rows, :LANES], keys) * scale + spread(foreign, some)
            at = lax.broadcasted_iota(jnp.int32, s.shape, 1)
            s = jnp.where(at < used[slot] - begin, s, -jnp.inf)
            old = top_ref[slot]
            peak = jnp.max(fold_lanes(s, jnp.maximum), axis=1, keepdims=True)
            new_top = jnp.maximum(old, jnp.ceil(peak))
            shrink = jnp.exp2(old - new_top)
            w = jnp.exp2(s - spread(new_top, some))
            top_ref[slot] = new_top
            total_ref[slot] = total_ref[slot] * shrink + jnp.sum(
                fold_lanes(w, jnp.add), axis=1, keepdims=True
            )
            acc_ref[slot] = acc_ref[slot] * shrink + jnp.dot(
                w.astype(BF16), values, preferred_element_type=F32
            )
            return carry

        lax.fori_loop(0, (used[slot] + some - 1) // some, visit, 0)

    for r in range(count):
        pl.when(out_of_range(total_ref[r]))(functools.partial(with_running_top, r))


def suffix_partials(
    queries, keys, values, new_keys, new_values, lengths, slot_row, after, span, kv, scale
):
    steps, _, heads, head_dim = queries.shape
    first, count = span[0], span[1] - span[0]
    cached = keys.shape[1]
    piece = math.gcd(cached, 2048)
    rows = steps * heads
    scalars = pl.BlockSpec(memory_space=pltpu.SMEM)
    away = pl.BlockSpec(memory_space=pl.ANY)
    inside = pl.BlockSpec(memory_space=pltpu.VMEM)
    shape = jax.ShapeDtypeStruct((3, count, rows, LANES), F32)
    return pl.pallas_call(
        functools.partial(suffix_kernel, kv, scale, first),
        in_specs=[scalars, scalars, inside, inside, inside, away, away, away],
        out_shape=shape,
        scratch_shapes=[
            pltpu.VMEM((count, 2 * rows, 2 * head_dim), BF16),
            pltpu.VMEM((2 * rows, piece // 2), F32),
            pltpu.VMEM((count, cached, head_dim), BF16),
            pltpu.VMEM((count, cached, head_dim), BF16),
            pltpu.SemaphoreType.DMA((count, cached // piece)),
            pltpu.SemaphoreType.DMA((count, cached // piece)),
        ],
        compiler_params=pltpu.CompilerParams(vmem_limit_bytes=GRANT if first else WIDE_GRANT),
        cost_estimate=pl.CostEstimate(
            flops=4 * count * rows * cached * head_dim,
            bytes_accessed=4 * count * cached * head_dim,
            transcendentals=count * rows * cached,
        ),
        name="suffix",
    )(lengths, slot_row, queries, new_keys, new_values, keys, values, after)


def combine_kernel(kv, parts_ref, *refs):
    near, out_ref = refs[:-1], refs[-1]
    steps, slots, heads, _ = out_ref.shape
    sources, height, width = parts_ref.shape
    per = height - STATS
    group = heads // kv

    wanted = lax.broadcasted_iota(jnp.int32, (STATS, 2 * width), 0)
    column = lax.broadcasted_iota(jnp.int32, (STATS, 2 * width), 1)
    head = (column % width) // LANES
    is_top = column < width
    picks = (is_top & (wanted == head)) | (
        jnp.logical_not(is_top) & ((wanted == 2 + head) | (wanted == 4 + head))
    )
    stats = jnp.concatenate([parts_ref[s, per:, :LANES] for s in range(sources)], axis=1)
    stats = lax.dot_general(
        stats,
        picks.astype(F32).astype(BF16),
        (((0,), (0,)), ((), ())),
        preferred_element_type=F32,
    )

    def own(kind):
        rows = []
        for t in range(steps):
            for r in range(slots):
                held, index = divmod(r, near[0].shape[1])
                x = near[held]
                at = [(h * steps + t) * group for h in range(kv)]
                rows.append(jnp.concatenate([x[kind, index, a : a + group] for a in at], axis=1))
        return jnp.concatenate(rows, axis=0)

    sums, tops, totals = [own(0)], [own(1)], [own(2)]
    for s in range(sources):
        at = slice(s * LANES, s * LANES + per)
        sums.append(parts_ref[s, :per, :].astype(F32))
        tops.append(stats[at, :width])
        totals.append(stats[at, width:])
    peak = functools.reduce(jnp.maximum, tops)
    factors = [jnp.exp2(m - peak) for m in tops]
    total = sum(f * x for f, x in zip(factors, totals))
    done = sum(f * x for f, x in zip(factors, sums)) / total
    for t in range(steps):
        for r in range(slots):
            at = (t * slots + r) * group
            both = [done[at : at + group, h * LANES : (h + 1) * LANES] for h in range(kv)]
            out_ref[t, r] = jnp.concatenate(both, axis=0).astype(BF16)


def combine(parts, near, kv, shape):
    return pl.pallas_call(
        functools.partial(combine_kernel, kv),
        out_shape=jax.ShapeDtypeStruct(shape, BF16),
        compiler_params=pltpu.CompilerParams(vmem_limit_bytes=16 * 1024 * 1024),
        name="combine",
    )(parts, *near)


def per_device(
    sources,
    queries,
    prefix_keys,
    prefix_values,
    suffix_keys,
    suffix_values,
    new_keys,
    new_values,
    suffix_lengths,
    slot_row,
):
    head_dim = queries.shape[-1]
    kv = prefix_keys.shape[1]
    scale = LOG2E / math.sqrt(head_dim)
    interleaved = lambda x: x.reshape(*x.shape[:-3], x.shape[-3] * x.shape[-2], x.shape[-1])

    def exchange(x):
        return lax.all_to_all(x, "wide", 0, 0, tiled=True)

    everyone = exchange(jnp.broadcast_to(queries[None], (sources, *queries.shape)))
    own = (
        queries,
        interleaved(suffix_keys),
        interleaved(suffix_values),
        new_keys,
        new_values,
        suffix_lengths,
        slot_row,
    )
    slots = queries.shape[1]
    early = suffix_partials(*own, suffix_lengths, (0, slots // 2), kv, scale)
    partials = prompt_partials(everyone, interleaved(prefix_keys), interleaved(prefix_values), early, kv, scale)
    home = exchange(partials)
    late = suffix_partials(*own, partials, (slots // 2, slots), kv, scale)
    return combine(home, [early, late], kv, queries.shape)


def solution(mesh):
    placed = (
        P(None, "wide", "tensor", None),
        P("wide", "tensor", None),
        P("wide", "tensor", None),
        P("wide", None, "tensor", None),
        P("wide", None, "tensor", None),
        P(None, "wide", "tensor", None),
        P(None, "wide", "tensor", None),
        P(),
        P("wide"),
    )
    return jax.shard_map(
        functools.partial(per_device, mesh.shape["wide"]),
        mesh=mesh,
        in_specs=placed,
        out_specs=P(None, "wide", "tensor", None),
        check_vma=False,
    )
```

profile of v0, /device:TPU:0, one launch (start us, length us, event | category | flops | bytes accessed | tf_op | source)
XLA Modules:
  0.0 200.6 jit_solution(9147743787468465366)
XLA Ops:
  0.0 1.5 broadcast_in_dim.2
  1.5 7.3 %all-to-all-start = ((bf16[8,2,4,16,128]{4,3,2,1,0:T(8,128)(2,1)}), bf16[8,2,4,16,128]{4,3,2,1,0:T(8,128)(2,1)S(1)}, u32[]{:S(2)}, u32[]{:S(2)}) async-start(bf16[8,2,4,16,128]{4,3,2,1,0:T(8,128)(2,1)} %broadcast_in_dim.2), calls=%async_computation | async-start | bytes 524288 | tf_op jit(solution)/shard_map/all_to_all | solution.py:508
  8.8 7.2 %suffix.2.refs_3_.refs_0_ = f32[3,2,32,128]{3,2,1,0:T(8,128)} custom-call(s32[32]{0:T(128)} %lengths.3, s32[4]{0:T(128)} %slots.3, bf16[2,4,16,128]{3,2,1,0:T(8,128)(2,1)} %refs_0_.3, bf16[2,4,2,128]{3,2,1,0:T(2,128)(2,1)} %refs_1_.3, bf16[2,4,2,128]{3,2,1,0:T(2,128)(2,1)} %refs_2_.3, bf16[4,8192,128]{2,1,0:T(8,128)(2,1)} %bitcast.4, ...), custom_call_target="tpu_custom_call" | custom-call | flops 268435456 | bytes 8388608 | tf_op jit(solution)/shard_map/suffix/pallas_call | solution.py:410
  16.0 1.7 all-to-all-done.refs_0_
  17.7 0.0 copy-start
  17.7 0.9 copy-done
  18.6 0.0 copy-start.2
  18.6 0.0 copy-start.3
  18.6 0.0 copy-start.4
  18.6 0.0 copy-start.5
  18.6 0.0 copy-start.6
  18.6 159.0 %prompt.1.refs_5_ = bf16[8,80,256]{2,1,0:T(8,128)(2,1)} custom-call(bf16[8,2,4,16,128]{4,3,2,1,0:T(8,128)(2,1)S(1)} %all-to-all-done.refs_0_, bf16[32768,128]{1,0:T(8,128)(2,1)} %bitcast.8, bf16[32768,128]{1,0:T(8,128)(2,1)} %bitcast.9, f32[3,2,32,128]{3,2,1,0:T(8,128)S(1)} %copy-done), custom_call_target="tpu_custom_call" | custom-call | flops 17179869184 | bytes 16777216 | tf_op jit(solution)/shard_map/prompt/pallas_call | solution.py:235
  177.6 13.1 %all-to-all-start.1 = ((bf16[8,80,256]{2,1,0:T(8,128)(2,1)}), bf16[8,80,256]{2,1,0:T(8,128)(2,1)S(1)}, u32[]{:S(2)}, u32[]{:S(2)}) async-start(bf16[8,80,256]{2,1,0:T(8,128)(2,1)} %prompt.1.refs_5_), calls=%async_computation.1 | async-start | bytes 655360 | tf_op jit(solution)/shard_map/all_to_all | solution.py:508
  190.8 0.0 copy-done.2
  190.8 0.0 copy-done.3
  190.8 0.0 copy-done.4
  190.8 0.0 copy-done.5
  190.8 0.0 copy-done.6
  190.8 0.0 copy-start.1
  190.8 3.6 %suffix.3.refs_1_ = f32[3,2,32,128]{3,2,1,0:T(8,128)S(1)} custom-call(s32[32]{0:T(128)S(1)} %copy-done.5, s32[4]{0:T(128)S(1)} %copy-done.6, bf16[2,4,16,128]{3,2,1,0:T(8,128)(2,1)S(1)} %copy-done.2, bf16[2,4,2,128]{3,2,1,0:T(2,128)(2,1)S(1)} %copy-done.3, bf16[2,4,2,128]{3,2,1,0:T(2,128)(2,1)S(1)} %copy-done.4, bf16[4,8192,128]{2,1,0:T(8,128)(2,1)} %bitcast.5, ...), custom_call_target="tpu_custom_call" | custom-call | flops 268435456 | bytes 8388608 | tf_op jit(solution)/shard_map/suffix/pallas_call | solution.py:410
  194.4 5.0 %all-to-all-done.1.parts_ref = bf16[8,80,256]{2,1,0:T(8,128)(2,1)S(1)} async-done(((bf16[8,80,256]{2,1,0:T(8,128)(2,1)}), bf16[8,80,256]{2,1,0:T(8,128)(2,1)S(1)}, u32[]{:S(2)}, u32[]{:S(2)}) %all-to-all-start.1) | async-done | bytes 327712 | tf_op jit(solution)/shard_map/all_to_all | solution.py:508
  199.4 0.0 copy-done.1
  199.4 1.2 combine.1
Async XLA Ops:
  1.5 16.2 %all-to-all-start = ((bf16[8,2,4,16,128]{4,3,2,1,0:T(8,128)(2,1)}), bf16[8,2,4,16,128]{4,3,2,1,0:T(8,128)(2,1)S(1)}, u32[]{:S(2)}, u32[]{:S(2)}) async-start(bf16[8,2,4,16,128]{4,3,2,1,0:T(8,128)(2,1)} %broadcast_in_dim.2), calls=%async_computation | async-start | bytes 524288 | tf_op jit(solution)/shard_map/all_to_all | solution.py:508
  17.7 0.9 copy-start
  18.6 172.2 %copy-start.2 = (bf16[2,4,16,128]{3,2,1,0:T(8,128)(2,1)S(1)}, bf16[2,4,16,128]{3,2,1,0:T(8,128)(2,1)}, u32[]{:S(2)}) copy-start(bf16[2,4,16,128]{3,2,1,0:T(8,128)(2,1)} %refs_0_.3) | copy-start | bytes 98308
  18.6 172.2 %copy-start.3 = (bf16[2,4,2,128]{3,2,1,0:T(2,128)(2,1)S(1)}, bf16[2,4,2,128]{3,2,1,0:T(2,128)(2,1)}, u32[]{:S(2)}) copy-start(bf16[2,4,2,128]{3,2,1,0:T(2,128)(2,1)} %refs_1_.3) | copy-start | bytes 12292
  18.6 172.2 %copy-start.4 = (bf16[2,4,2,128]{3,2,1,0:T(2,128)(2,1)S(1)}, bf16[2,4,2,128]{3,2,1,0:T(2,128)(2,1)}, u32[]{:S(2)}) copy-start(bf16[2,4,2,128]{3,2,1,0:T(2,128)(2,1)} %refs_2_.3) | copy-start | bytes 12292
  18.6 172.2 %copy-start.5 = (s32[32]{0:T(128)S(1)}, s32[32]{0:T(128)}, u32[]{:S(2)}) copy-start(s32[32]{0:T(128)} %lengths.3) | copy-start | bytes 388
  18.6 172.2 %copy-start.6 = (s32[4]{0:T(128)S(1)}, s32[4]{0:T(128)}, u32[]{:S(2)}) copy-start(s32[4]{0:T(128)} %slots.3) | copy-start | bytes 52
  177.6 21.8 %all-to-all-start.1 = ((bf16[8,80,256]{2,1,0:T(8,128)(2,1)}), bf16[8,80,256]{2,1,0:T(8,128)(2,1)S(1)}, u32[]{:S(2)}, u32[]{:S(2)}) async-start(bf16[8,80,256]{2,1,0:T(8,128)(2,1)} %prompt.1.refs_5_), calls=%async_computation.1 | async-start | bytes 655360 | tf_op jit(solution)/shard_map/all_to_all | solution.py:508
  190.8 8.6 %copy-start.1 = (f32[3,2,32,128]{3,2,1,0:T(8,128)S(1)}, f32[3,2,32,128]{3,2,1,0:T(8,128)}, u32[]{:S(2)}) copy-start(f32[3,2,32,128]{3,2,1,0:T(8,128)} %suffix.2.refs_3_.refs_0_) | copy-start | bytes 294916
where the time goes:
time: 204 us; the launch traced here: 201 us
  Pallas kernels  171 us (84%)
  starting transfers between devices  20.4 us (10%)
  waiting for transfers between devices  6.71 us (3%)
  local copies, waits for them, and re-layouts  2.44 us (1%)
    pallas_call x1, Pallas kernels, prompt_partials(): pl.pallas_call(functools.partial(prompt_kernel, kv, piece, scale), in_spe...  159 us
    all_to_all x2, starting transfers between devices, exchange(): return lax.all_to_all(x, 'wide', 0, 0, tiled=True)  20.4 us
    pallas_call x2, Pallas kernels, suffix_partials(): pl.pallas_call(functools.partial(suffix_kernel, kv, scale, first), in_spe...  10.8 us
    all_to_all x2, waiting for transfers between devices, exchange(): return lax.all_to_all(x, 'wide', 0, 0, tiled=True)  6.71 us
  transfers between devices with their start and end apart: 2, of which 2 were waited for; matrix products, arithmetic and copies ran while one was open for 0% of the time, Pallas kernels for 5%

commit v1 on v0

--- a/solution.py
+++ b/solution.py
@@ -12,7 +12,7 @@
 LANES = 128
 STEPS = 2
 TILE, BAND, MAX_WAVE, STATS = 256, 64, 1024, 16
-WIDE_GRANT, GRANT = 57 * 1024 * 1024, 50 * 1024 * 1024
+GRANT = 50 * 1024 * 1024
 UNROLL, LAG = 8, 1
 TOO_LARGE, TOO_SMALL = 2.0**100, 2.0**-60
 F32 = jnp.float32
@@ -205,21 +205,27 @@
 
     pl.when(out_of_range(acc[:, LANES:]))(with_running_top)
 
-    def as_rows(x):
+    lane = lax.broadcasted_iota(jnp.int32, (per, LANES), 1)
+
+    def as_rows(columns):
+        tile = jnp.zeros((per, LANES), F32)
+        for i in range(kv * sources):
+            tile = jnp.where(lane == i, columns(slice(i * per, (i + 1) * per)), tile)
         rest = jnp.zeros((LANES - per, LANES), F32)
-        return jnp.concatenate([x, rest], axis=0).T[:STATS]
-
+        return jnp.concatenate([tile, rest], axis=0).T
+
+    tops = as_rows(lambda at: top[at, :])
+    sums = as_rows(lambda at: acc[at, LANES:])
+    high = sums.astype(BF16).astype(F32)
     row = lax.broadcasted_iota(jnp.int32, (STATS, LANES), 0)
     for s in range(sources):
         stats = jnp.zeros((STATS, LANES), F32)
         for h in range(kv):
-            at = slice(h * rows_head + s * per, h * rows_head + (s + 1) * per)
+            i = h * sources + s
+            at = slice(i * per, (i + 1) * per)
             out_ref[s, :per, h * LANES : (h + 1) * LANES] = acc[at, :LANES].astype(BF16)
-            sums = as_rows(acc[at, LANES:])
-            high = sums.astype(BF16).astype(F32)
-            stats = jnp.where(row == h, as_rows(top[at, :]), stats)
-            stats = jnp.where(row == 2 + h, high, stats)
-            stats = jnp.where(row == 4 + h, sums - high, stats)
+            for k, kind in enumerate((tops, high, sums - high)):
+                stats = jnp.where(row == 2 * k + h, kind[i : i + 1], stats)
         rest = [jnp.zeros_like(stats)] * (kv - 1)
         out_ref[s, per:, :] = jnp.concatenate([stats, *rest], axis=1).astype(BF16)
 
@@ -419,7 +425,7 @@
             pltpu.SemaphoreType.DMA((count, cached // piece)),
             pltpu.SemaphoreType.DMA((count, cached // piece)),
         ],
-        compiler_params=pltpu.CompilerParams(vmem_limit_bytes=GRANT if first else WIDE_GRANT),
+        compiler_params=pltpu.CompilerParams(vmem_limit_bytes=GRANT),
         cost_estimate=pl.CostEstimate(
             flops=4 * count * rows * cached * head_dim,
             bytes_accessed=4 * count * cached * head_dim,
@@ -455,8 +461,8 @@
         rows = []
         for t in range(steps):
             for r in range(slots):
-                held, index = divmod(r, near[0].shape[1])
-                x = near[held]
+                early = near[0].shape[1]
+                x, index = (near[0], r) if r < early else (near[1], r - early)
                 at = [(h * steps + t) * group for h in range(kv)]
                 rows.append(jnp.concatenate([x[kind, index, a : a + group] for a in at], axis=1))
         return jnp.concatenate(rows, axis=0)
@@ -518,10 +524,10 @@
         slot_row,
     )
     slots = queries.shape[1]
-    early = suffix_partials(*own, suffix_lengths, (0, slots // 2), kv, scale)
+    early = suffix_partials(*own, suffix_lengths, (0, slots // 4), kv, scale)
     partials = prompt_partials(everyone, interleaved(prefix_keys), interleaved(prefix_values), early, kv, scale)
     home = exchange(partials)
-    late = suffix_partials(*own, partials, (slots // 2, slots), kv, scale)
+    late = suffix_partials(*own, partials, (slots // 4, slots), kv, scale)
     return combine(home, [early, late], kv, queries.shape)
 
 

time: 204 us -> 207 us (1.015)
  the two profiles are of different devices: /device:TPU:0 before, /device:TPU:28 now
where the time goes in v1:
time: 207 us; the launch traced here: 204 us
  Pallas kernels  182 us (88%)
  starting transfers between devices  15.4 us (7%)
  local copies, waits for them, and re-layouts  4.96 us (2%)
    pallas_call x1, Pallas kernels, prompt_partials(): pl.pallas_call(functools.partial(prompt_kernel, kv, piece, scale), in_spe...  159 us
    pallas_call x2, Pallas kernels, suffix_partials(): pl.pallas_call(functools.partial(suffix_kernel, kv, scale, first), in_spe...  22.4 us
    all_to_all x2, starting transfers between devices, exchange(): return lax.all_to_all(x, 'wide', 0, 0, tiled=True)  15.4 us
  transfers between devices with their start and end apart: 2, of which 1 were waited for; matrix products, arithmetic and copies ran while one was open for 0% of the time, Pallas kernels for 11%

profile of v1, /device:TPU:28, one launch (start us, length us, event | category | flops | bytes accessed | tf_op | source)
XLA Modules:
  0.0 203.6 jit_solution(16353035192065568067)
XLA Ops:
  0.0 1.5 broadcast_in_dim.2
  1.5 6.0 %all-to-all-start = ((bf16[8,2,4,16,128]{4,3,2,1,0:T(8,128)(2,1)}), bf16[8,2,4,16,128]{4,3,2,1,0:T(8,128)(2,1)S(1)}, u32[]{:S(2)}, u32[]{:S(2)}) async-start(bf16[8,2,4,16,128]{4,3,2,1,0:T(8,128)(2,1)} %broadcast_in_dim.2), calls=%async_computation | async-start | bytes 524288 | tf_op jit(solution)/shard_map/all_to_all | solution.py:514
  7.5 0.0 copy-start
  7.5 0.8 copy-done
  8.3 0.0 copy-start.2
  8.3 0.7 copy-done.2
  8.9 0.0 copy-start.4
  9.0 0.7 copy-done.4
  9.6 0.0 copy-start.6
  9.6 0.7 copy-done.6
  10.3 0.7 copy-done.8
  10.9 2.3 %suffix.2.refs_3_.refs_0_ = f32[3,1,32,128]{3,2,1,0:T(8,128)S(1)} custom-call(s32[32]{0:T(128)S(1)} %copy-done.6, s32[4]{0:T(128)S(1)} %copy-done.8, bf16[2,4,16,128]{3,2,1,0:T(8,128)(2,1)S(1)} %copy-done, bf16[2,4,2,128]{3,2,1,0:T(2,128)(2,1)S(1)} %copy-done.2, bf16[2,4,2,128]{3,2,1,0:T(2,128)(2,1)S(1)} %copy-done.4, bf16[4,8192,128]{2,1,0:T(8,128)(2,1)} %bitcast.4, ...), custom_call_target="tpu_custom_call" | custom-call | flops 134217728 | bytes 4194304 | tf_op jit(solution)/shard_map/suffix/pallas_call | solution.py:416
  13.3 0.7 all-to-all-done.refs_0_
  14.0 0.0 copy-start.9
  14.0 158.8 %prompt.1.refs_5_ = bf16[8,80,256]{2,1,0:T(8,128)(2,1)} custom-call(bf16[8,2,4,16,128]{4,3,2,1,0:T(8,128)(2,1)S(1)} %all-to-all-done.refs_0_, bf16[32768,128]{1,0:T(8,128)(2,1)} %bitcast.8, bf16[32768,128]{1,0:T(8,128)(2,1)} %bitcast.9, f32[3,1,32,128]{3,2,1,0:T(8,128)S(1)} %suffix.2.refs_3_.refs_0_), custom_call_target="tpu_custom_call" | custom-call | flops 17179869184 | bytes 16777216 | tf_op jit(solution)/shard_map/prompt/pallas_call | solution.py:241
  172.9 9.4 %all-to-all-start.1 = ((bf16[8,80,256]{2,1,0:T(8,128)(2,1)}), bf16[8,80,256]{2,1,0:T(8,128)(2,1)S(1)}, u32[]{:S(2)}, u32[]{:S(2)}) async-start(bf16[8,80,256]{2,1,0:T(8,128)(2,1)} %prompt.1.refs_5_), calls=%async_computation.1 | async-start | bytes 655360 | tf_op jit(solution)/shard_map/all_to_all | solution.py:514
  182.3 0.0 copy-done.1
  182.3 0.0 copy-done.3
  182.3 0.0 copy-done.5
  182.3 0.0 copy-done.7
  182.3 0.0 copy-done.9
  182.3 20.1 %suffix.3.refs_1_ = f32[3,3,32,128]{3,2,1,0:T(8,128)S(1)} custom-call(s32[32]{0:T(128)S(1)} %copy-done.7, s32[4]{0:T(128)S(1)} %copy-done.9, bf16[2,4,16,128]{3,2,1,0:T(8,128)(2,1)S(1)} %copy-done.1, bf16[2,4,2,128]{3,2,1,0:T(2,128)(2,1)S(1)} %copy-done.3, bf16[2,4,2,128]{3,2,1,0:T(2,128)(2,1)S(1)} %copy-done.5, bf16[4,8192,128]{2,1,0:T(8,128)(2,1)} %bitcast.5, ...), custom_call_target="tpu_custom_call" | custom-call | flops 402653184 | bytes 12582912 | tf_op jit(solution)/shard_map/suffix/pallas_call | solution.py:416
  202.4 0.0 all-to-all-done.1.parts_ref
  202.5 1.2 combine.1
  (5 shorter events, 0.0 us)
Async XLA Ops:
  1.5 12.5 %all-to-all-start = ((bf16[8,2,4,16,128]{4,3,2,1,0:T(8,128)(2,1)}), bf16[8,2,4,16,128]{4,3,2,1,0:T(8,128)(2,1)S(1)}, u32[]{:S(2)}, u32[]{:S(2)}) async-start(bf16[8,2,4,16,128]{4,3,2,1,0:T(8,128)(2,1)} %broadcast_in_dim.2), calls=%async_computation | async-start | bytes 524288 | tf_op jit(solution)/shard_map/all_to_all | solution.py:514
  7.5 0.8 copy-start
  8.3 0.7 copy-start.2
  8.9 0.7 copy-start.4
  9.6 0.7 copy-start.6
  10.3 0.7 copy-start.8
  14.0 168.3 %copy-start.1 = (bf16[2,4,16,128]{3,2,1,0:T(8,128)(2,1)S(1)}, bf16[2,4,16,128]{3,2,1,0:T(8,128)(2,1)}, u32[]{:S(2)}) copy-start(bf16[2,4,16,128]{3,2,1,0:T(8,128)(2,1)} %refs_0_.3) | copy-start | bytes 98308
  14.0 168.3 %copy-start.3 = (bf16[2,4,2,128]{3,2,1,0:T(2,128)(2,1)S(1)}, bf16[2,4,2,128]{3,2,1,0:T(2,128)(2,1)}, u32[]{:S(2)}) copy-start(bf16[2,4,2,128]{3,2,1,0:T(2,128)(2,1)} %refs_1_.3) | copy-start | bytes 12292
  14.0 168.3 %copy-start.5 = (bf16[2,4,2,128]{3,2,1,0:T(2,128)(2,1)S(1)}, bf16[2,4,2,128]{3,2,1,0:T(2,128)(2,1)}, u32[]{:S(2)}) copy-start(bf16[2,4,2,128]{3,2,1,0:T(2,128)(2,1)} %refs_2_.3) | copy-start | bytes 12292
  14.0 168.3 %copy-start.7 = (s32[32]{0:T(128)S(1)}, s32[32]{0:T(128)}, u32[]{:S(2)}) copy-start(s32[32]{0:T(128)} %lengths.3) | copy-start | bytes 388
  14.0 168.3 %copy-start.9 = (s32[4]{0:T(128)S(1)}, s32[4]{0:T(128)}, u32[]{:S(2)}) copy-start(s32[4]{0:T(128)} %slots.3) | copy-start | bytes 52
  172.9 29.6 %all-to-all-start.1 = ((bf16[8,80,256]{2,1,0:T(8,128)(2,1)}), bf16[8,80,256]{2,1,0:T(8,128)(2,1)S(1)}, u32[]{:S(2)}, u32[]{:S(2)}) async-start(bf16[8,80,256]{2,1,0:T(8,128)(2,1)} %prompt.1.refs_5_), calls=%async_computation.1 | async-start | bytes 655360 | tf_op jit(solution)/shard_map/all_to_all | solution.py:514

commit v2 on v1

--- a/solution.py
+++ b/solution.py
@@ -11,7 +11,7 @@
 LOG2E = 1.4426950408889634
 LANES = 128
 STEPS = 2
-TILE, BAND, MAX_WAVE, STATS = 256, 64, 1024, 16
+TILE, BAND, MAX_WAVE, STATS = 256, 32, 1024, 16
 GRANT = 50 * 1024 * 1024
 UNROLL, LAG = 8, 1
 TOO_LARGE, TOO_SMALL = 2.0**100, 2.0**-60

time: 207 us -> 318 us (1.54)
  the two profiles are of different devices: /device:TPU:28 before, /device:TPU:0 now
where the time goes in v2:
time: 318 us; the launch traced here: 316 us
  Pallas kernels  299 us (94%)
  starting transfers between devices  12.6 us (4%)
  local copies, waits for them, and re-layouts  4.97 us (2%)
    pallas_call x1, Pallas kernels, prompt_partials(): pl.pallas_call(functools.partial(prompt_kernel, kv, piece, scale), in_spe...  275 us
    pallas_call x2, Pallas kernels, suffix_partials(): pl.pallas_call(functools.partial(suffix_kernel, kv, scale, first), in_spe...  22.4 us
    all_to_all x2, starting transfers between devices, exchange(): return lax.all_to_all(x, 'wide', 0, 0, tiled=True)  12.6 us
  transfers between devices with their start and end apart: 2, of which 0 were waited for; matrix products, arithmetic and copies ran while one was open for 0% of the time, Pallas kernels for 7%

profile of v2, /device:TPU:0, one launch (start us, length us, event | category | flops | bytes accessed | tf_op | source)
XLA Modules:
  0.0 316.4 jit_solution(12536175547298785659)
XLA Ops:
  0.0 1.5 broadcast_in_dim.2
  1.5 7.3 %all-to-all-start = ((bf16[8,2,4,16,128]{4,3,2,1,0:T(8,128)(2,1)}), bf16[8,2,4,16,128]{4,3,2,1,0:T(8,128)(2,1)S(1)}, u32[]{:S(2)}, u32[]{:S(2)}) async-start(bf16[8,2,4,16,128]{4,3,2,1,0:T(8,128)(2,1)} %broadcast_in_dim.2), calls=%async_computation | async-start | bytes 524288 | tf_op jit(solution)/shard_map/all_to_all | solution.py:514
  8.8 0.8 copy-done
  9.5 0.7 copy-done.2
  10.2 0.7 copy-done.4
  10.9 0.7 copy-done.6
  11.6 0.7 copy-done.8
  12.2 9.9 %suffix.2.refs_3_.refs_0_ = f32[3,1,32,128]{3,2,1,0:T(8,128)S(1)} custom-call(s32[32]{0:T(128)S(1)} %copy-done.6, s32[4]{0:T(128)S(1)} %copy-done.8, bf16[2,4,16,128]{3,2,1,0:T(8,128)(2,1)S(1)} %copy-done, bf16[2,4,2,128]{3,2,1,0:T(2,128)(2,1)S(1)} %copy-done.2, bf16[2,4,2,128]{3,2,1,0:T(2,128)(2,1)S(1)} %copy-done.4, bf16[4,8192,128]{2,1,0:T(8,128)(2,1)} %bitcast.4, ...), custom_call_target="tpu_custom_call" | custom-call | flops 134217728 | bytes 4194304 | tf_op jit(solution)/shard_map/suffix/pallas_call | solution.py:416
  22.1 0.0 all-to-all-done.refs_0_
  22.2 0.0 copy-start.1
  22.2 0.0 copy-start.3
  22.2 0.0 copy-start.5
  22.2 0.0 copy-start.7
  22.2 0.0 copy-start.9
  22.2 275.2 %prompt.1.refs_5_ = bf16[8,80,256]{2,1,0:T(8,128)(2,1)} custom-call(bf16[8,2,4,16,128]{4,3,2,1,0:T(8,128)(2,1)S(1)} %all-to-all-done.refs_0_, bf16[32768,128]{1,0:T(8,128)(2,1)} %bitcast.8, bf16[32768,128]{1,0:T(8,128)(2,1)} %bitcast.9, f32[3,1,32,128]{3,2,1,0:T(8,128)S(1)} %suffix.2.refs_3_.refs_0_), custom_call_target="tpu_custom_call" | custom-call | flops 17179869184 | bytes 16777216 | tf_op jit(solution)/shard_map/prompt/pallas_call | solution.py:241
  297.4 5.3 %all-to-all-start.1 = ((bf16[8,80,256]{2,1,0:T(8,128)(2,1)}), bf16[8,80,256]{2,1,0:T(8,128)(2,1)S(1)}, u32[]{:S(2)}, u32[]{:S(2)}) async-start(bf16[8,80,256]{2,1,0:T(8,128)(2,1)} %prompt.1.refs_5_), calls=%async_computation.1 | async-start | bytes 655360 | tf_op jit(solution)/shard_map/all_to_all | solution.py:514
  302.7 0.0 copy-done.1
  302.7 0.0 copy-done.3
  302.7 0.0 copy-done.5
  302.7 0.0 copy-done.7
  302.7 0.0 copy-done.9
  302.7 12.5 %suffix.3.refs_1_ = f32[3,3,32,128]{3,2,1,0:T(8,128)S(1)} custom-call(s32[32]{0:T(128)S(1)} %copy-done.7, s32[4]{0:T(128)S(1)} %copy-done.9, bf16[2,4,16,128]{3,2,1,0:T(8,128)(2,1)S(1)} %copy-done.1, bf16[2,4,2,128]{3,2,1,0:T(2,128)(2,1)S(1)} %copy-done.3, bf16[2,4,2,128]{3,2,1,0:T(2,128)(2,1)S(1)} %copy-done.5, bf16[4,8192,128]{2,1,0:T(8,128)(2,1)} %bitcast.5, ...), custom_call_target="tpu_custom_call" | custom-call | flops 402653184 | bytes 12582912 | tf_op jit(solution)/shard_map/suffix/pallas_call | solution.py:416
  315.2 0.0 all-to-all-done.1.parts_ref
  315.2 1.2 combine.1
  (5 shorter events, 0.0 us)
Async XLA Ops:
  1.5 20.6 %all-to-all-start = ((bf16[8,2,4,16,128]{4,3,2,1,0:T(8,128)(2,1)}), bf16[8,2,4,16,128]{4,3,2,1,0:T(8,128)(2,1)S(1)}, u32[]{:S(2)}, u32[]{:S(2)}) async-start(bf16[8,2,4,16,128]{4,3,2,1,0:T(8,128)(2,1)} %broadcast_in_dim.2), calls=%async_computation | async-start | bytes 524288 | tf_op jit(solution)/shard_map/all_to_all | solution.py:514
  8.8 0.8 copy-start
  9.5 0.7 copy-start.2
  10.2 0.7 copy-start.4
  10.9 0.7 copy-start.6
  11.6 0.7 copy-start.8
  22.2 280.5 %copy-start.1 = (bf16[2,4,16,128]{3,2,1,0:T(8,128)(2,1)S(1)}, bf16[2,4,16,128]{3,2,1,0:T(8,128)(2,1)}, u32[]{:S(2)}) copy-start(bf16[2,4,16,128]{3,2,1,0:T(8,128)(2,1)} %refs_0_.3) | copy-start | bytes 98308
  22.2 280.5 %copy-start.3 = (bf16[2,4,2,128]{3,2,1,0:T(2,128)(2,1)S(1)}, bf16[2,4,2,128]{3,2,1,0:T(2,128)(2,1)}, u32[]{:S(2)}) copy-start(bf16[2,4,2,128]{3,2,1,0:T(2,128)(2,1)} %refs_1_.3) | copy-start | bytes 12292
  22.2 280.5 %copy-start.5 = (bf16[2,4,2,128]{3,2,1,0:T(2,128)(2,1)S(1)}, bf16[2,4,2,128]{3,2,1,0:T(2,128)(2,1)}, u32[]{:S(2)}) copy-start(bf16[2,4,2,128]{3,2,1,0:T(2,128)(2,1)} %refs_2_.3) | copy-start | bytes 12292
  22.2 280.5 %copy-start.7 = (s32[32]{0:T(128)S(1)}, s32[32]{0:T(128)}, u32[]{:S(2)}) copy-start(s32[32]{0:T(128)} %lengths.3) | copy-start | bytes 388
  22.2 280.5 %copy-start.9 = (s32[4]{0:T(128)S(1)}, s32[4]{0:T(128)}, u32[]{:S(2)}) copy-start(s32[4]{0:T(128)} %slots.3) | copy-start | bytes 52
  297.4 17.8 %all-to-all-start.1 = ((bf16[8,80,256]{2,1,0:T(8,128)(2,1)}), bf16[8,80,256]{2,1,0:T(8,128)(2,1)S(1)}, u32[]{:S(2)}, u32[]{:S(2)}) async-start(bf16[8,80,256]{2,1,0:T(8,128)(2,1)} %prompt.1.refs_5_), calls=%async_computation.1 | async-start | bytes 655360 | tf_op jit(solution)/shard_map/all_to_all | solution.py:514
